TPU v7x, 32 devices: a whole 2x2x4 slice. The times are simulated.
32 devices in a mesh: dp: 8 (over z, y), order: 4 (over x, core).
Axes of the slice: x: 2, y: 2, z: 4, core: 2. Of those that a mesh axis runs over, the one named last changes fastest.
Arguments:
- images: bfloat16 [1024, 128, 512], P(('dp', 'order')), may hold values from -6 to 6
- radial_interp: bfloat16 [128, 128], replicated, may hold values from -0.5 to 0.5
- assignment: int32 [256], replicated, may hold values from 0 to 255, as said below
- counts: int32 [256], P('order'), may hold values from 32 to 128, as said below
- radial_basis: bfloat16 [256, 128, 128], P('order'), may hold values from -0.5 to 0.5
- eigenbasis: bfloat16 [256, 128, 128], P('order'), may hold values from -0.5 to 0.5
Outputs:
- covariance: float32 [256, 32768], P(('order', 'dp'))
- projected: bfloat16 [2, 256, 1024, 128], P(None, 'order', 'dp')
Inputs may be any that keep to these rules, and one draw needn't show every extreme that they name: `assignment`: a permutation of the orders 0 to 255. The slot of order 0 keeps 128; the slot of order 256 - 1 keeps 32; counts fall with the order up to a jitter of 3.
All inputs are finite; a program needn't handle non-finite values.
Results may differ from a plain program's by a relative error of at most 0.013.
Values may be sent and summed in bfloat16 or wider, within the bound.
A program may use at most 128 MiB of HBM per device.

v0:
```python
import functools
import math

import jax
import jax.numpy as jnp
import ml_dtypes
import numpy as np
from jax import lax
from jax.experimental import pallas as pl
from jax.experimental.pallas import tpu as pltpu
from jax.sharding import PartitionSpec as P

MESH = pl.DeviceIdType.MESH
BF16 = jnp.bfloat16
F32 = jnp.float32
CORES = 2
WINDOW = 4


def base_table(orders, samples):
    angle = (np.arange(orders)[:, None] * np.arange(samples)[None, :]) % samples
    theta = angle.astype(np.float32) * np.float32(2.0 * math.pi / samples)
    rows = np.concatenate([np.cos(theta), -np.sin(theta)], 0) / np.sqrt(np.float32(samples))
    return rows.astype(ml_dtypes.bfloat16)


def kernel(
    n_order, n_dp, images_hbm, interp, row_index, base, mask, basis_hbm, eigen_hbm,
    cov_out, proj_out,
    images, basis, eigen, table, kept, wide, send, recv, proj, cov_own, cov_y, cov_z, cov_got,
    cov_rows, image_sem, weight_sem, spec_send, spec_recv, y_send, y_recv, z_send, z_recv, proj_sem,
):
    local_images, nodes, samples = images.shape
    slots = basis.shape[0]
    chips, half, per_dp = n_order // CORES, n_dp // 2, slots // n_dp
    chip_rows = CORES * slots * 2
    block = 2 * n_dp * local_images
    me, my_dp = lax.axis_index("order"), lax.axis_index("dp")
    my_chip, my_core = me // CORES, me % CORES
    my_z, my_y = my_dp // 2, my_dp % 2

    def order_of(dx, dc):
        return lax.rem(my_chip + dx, chips) * CORES + lax.rem(my_core + dc, CORES)

    peers = [(dx, dc) for dx in range(1, chips) for dc in range(CORES)] + [(0, 1)]
    y_peer = my_z * 2 + (1 - my_y)

    def z_peer(q):
        return lax.rem(my_z + q, half)

    barrier = pltpu.get_barrier_semaphore()
    for dx, dc in peers:
        pl.semaphore_signal(barrier, 1, device_id={"order": order_of(dx, dc)}, device_id_type=MESH)
    pl.semaphore_signal(barrier, 1, device_id={"dp": y_peer}, device_id_type=MESH)
    for q in range(1, half):
        pl.semaphore_signal(
            barrier, 1, device_id={"dp": z_peer(q) * 2 + my_y}, device_id_type=MESH
        )

    parts = image_sem.shape[0]
    per_part = local_images // parts
    image_copies = [
        pltpu.make_async_copy(
            images_hbm.at[pl.ds(n * per_part, per_part)],
            images.at[pl.ds(n * per_part, per_part)],
            image_sem.at[n],
        )
        for n in range(parts)
    ]
    for copy in image_copies:
        copy.start()
    basis_copy = pltpu.make_async_copy(basis_hbm, basis, weight_sem.at[0])
    eigen_copy = pltpu.make_async_copy(eigen_hbm, eigen, weight_sem.at[1])
    basis_copy.start()
    eigen_copy.start()

    total_rows = table.shape[0]
    for r in range(0, total_rows, 128):
        hot = row_index[pl.ds(r, 128), :] == lax.broadcasted_iota(
            jnp.int32, (128, base.shape[0]), 1
        )
        table[pl.ds(r, 128), :] = jnp.dot(
            hot.astype(F32).astype(BF16), base[...], preferred_element_type=F32
        ).astype(BF16)

    def transform(dx, first):
        start = pl.multiple_of(lax.rem(my_chip + dx, chips) * chip_rows, chip_rows)
        for n in range(parts):
            if first:
                image_copies[n].wait()

            @pl.loop(0, per_part // 2)
            def _(h):
                i = n * per_part + h * 2
                pair = images[pl.ds(i, 2)].reshape(2 * nodes, samples)
                got = lax.dot_general(
                    table[pl.ds(start, chip_rows), :], pair,
                    (((1,), (1,)), ((), ())), preferred_element_type=F32,
                )
                wide[pl.ds(i, chip_rows, stride=local_images), :] = got[:, :nodes]
                wide[pl.ds(i + 1, chip_rows, stride=local_images), :] = got[:, nodes:]

    def spec_copy(k, t):
        dx, dc = peers[t]
        return pltpu.make_async_remote_copy(
            src_ref=send.at[t, k],
            dst_ref=recv.at[k, me],
            send_sem=spec_send.at[t, k],
            recv_sem=spec_recv.at[t, k],
            device_id={"order": order_of(dx, dc)},
            device_id_type=MESH,
        )

    def rows_of(dc, k):
        return pl.ds(
            pl.multiple_of((lax.rem(my_core + dc, CORES) * per_dp + k) * block, block), block
        )

    far = len(peers) - 1
    for dx in range(1, chips):
        transform(dx, dx == 1)
        if dx == 1:
            pl.semaphore_wait(barrier, len(peers) + half)
        for k in range(per_dp):
            for dc in range(CORES):
                t = (dx - 1) * CORES + dc
                send[t, k] = wide[rows_of(dc, k), :].astype(BF16)
                if k < WINDOW:
                    spec_copy(k, t).start()
    transform(0, chips == 1)
    for k in range(per_dp):
        send[far, k] = wide[rows_of(1, k), :].astype(BF16)
        spec_copy(k, far).start()
    for k in range(per_dp):
        recv[k, me] = wide[rows_of(0, k), :].astype(BF16)

    basis_copy.wait()

    @pl.loop(0, slots)
    def _(j):
        kept[j] = (
            jnp.dot(interp[...], basis[j], preferred_element_type=F32) * mask[j]
        ).astype(BF16)

    eigen_copy.wait()
    scale = 1.0 / (local_images * n_order * n_dp)

    def y_copy(k):
        return pltpu.make_async_remote_copy(
            src_ref=cov_own.at[k, 1 - my_y],
            dst_ref=cov_y.at[k],
            send_sem=y_send.at[k],
            recv_sem=y_recv.at[k],
            device_id={"dp": y_peer},
            device_id_type=MESH,
        )

    def z_copy(k, q):
        return pltpu.make_async_remote_copy(
            src_ref=cov_z.at[k, z_peer(q)],
            dst_ref=cov_got.at[k, q],
            send_sem=z_send.at[k, q],
            recv_sem=z_recv.at[k, q],
            device_id={"dp": z_peer(q) * 2 + my_y},
            device_id_type=MESH,
        )

    def proj_copy(k):
        return pltpu.make_async_copy(proj.at[k], proj_out.at[:, :, k], proj_sem.at[k])

    def slot_work(k):
        @pl.loop(0, half)
        def _(z):
            for y in range(2):
                d = z * 2 + y
                j = d * per_dp + k
                at = pl.multiple_of(d * 2 * local_images, 2 * local_images)
                got = recv[k, :, pl.ds(at, 2 * local_images), :]
                both = jnp.concatenate(
                    [got[:, :local_images], got[:, local_images:]], 0
                ).reshape(2 * n_order * local_images, nodes)
                coef = jnp.dot(both, kept[j], preferred_element_type=F32).astype(BF16)
                real, imag = coef[: n_order * local_images], coef[n_order * local_images :]
                mixed = jnp.concatenate([real - imag, real + imag], 0)
                cov = lax.dot_general(
                    coef, mixed, (((0,), (0,)), ((), ())), preferred_element_type=F32
                )
                cov_own[k, y, z] = (cov * scale).astype(BF16)
                out = jnp.dot(coef, eigen[j], preferred_element_type=F32).astype(BF16)
                proj[k, 0, d] = out[: n_order * local_images]
                proj[k, 1, d] = out[n_order * local_images :]

    def reduce_y(k):
        y_copy(k).wait_recv()
        cov_z[k] = (cov_own[k, my_y].astype(F32) + cov_y[k].astype(F32)).astype(BF16)
        for q in range(1, half):
            z_copy(k, q).start()

    def reduce_z(k):
        whole = cov_z[k, my_z].astype(F32)
        for q in range(1, half):
            z_copy(k, q).wait_recv()
            whole = whole + cov_got[k, q].astype(F32)
        flipped = whole.T
        width = whole.shape[0]
        cov_rows[pl.ds(k, width, stride=per_dp), :] = (whole + flipped) * 0.5
        cov_rows[pl.ds(width * per_dp + k, width, stride=per_dp), :] = (whole - flipped) * 0.5

    for k in range(per_dp):
        if k + WINDOW < per_dp:
            for t in range(far):
                spec_copy(k + WINDOW, t).start()
        for t in range(len(peers)):
            spec_copy(k, t).wait_recv()
        slot_work(k)
        y_copy(k).start()
        proj_copy(k).start()
        if k >= 1:
            reduce_y(k - 1)
        if k >= 2:
            reduce_z(k - 2)
    reduce_y(per_dp - 1)
    for k in range(max(0, per_dp - 2), per_dp):
        reduce_z(k)
    for r in range(cov_rows.shape[0] // per_dp):
        cov_out[:, pl.ds(r * 128, 128)] = cov_rows[pl.ds(r * per_dp, per_dp), :]
    for k in range(per_dp):
        for t in range(len(peers)):
            spec_copy(k, t).wait_send()
        y_copy(k).wait_send()
        for q in range(1, half):
            z_copy(k, q).wait_send()
        proj_copy(k).wait()


def body(n_order, n_dp, images, radial_interp, assignment, counts, radial_basis, eigenbasis):
    local_images, nodes, samples = images.shape
    slot_total = assignment.shape[0]
    slots, _, width = radial_basis.shape
    per_dp, half, chips = slots // n_dp, n_dp // 2, n_order // CORES
    placed = assignment.reshape(n_order, n_dp, per_dp).transpose(0, 2, 1)
    row_index = (
        placed[..., None] + slot_total * jnp.arange(2, dtype=jnp.int32)
    ).reshape(2 * slot_total, 1)
    mask = (jnp.arange(width, dtype=jnp.int32)[None, :] < counts[:, None]).astype(F32)
    mask = mask.reshape(slots, 1, width)
    base = jnp.asarray(base_table(slot_total, samples))
    block = 2 * n_dp * local_images
    n_peers = n_order - 1
    chip_rows = CORES * slots * 2
    parts = 4
    vmem = pl.BlockSpec(memory_space=pltpu.VMEM)
    any_space = pl.BlockSpec(memory_space=pl.ANY)
    dma = pltpu.SemaphoreType.DMA
    group = n_order * local_images
    covariance, projected = pl.pallas_call(
        functools.partial(kernel, n_order, n_dp),
        out_shape=(
            jax.ShapeDtypeStruct((per_dp, 2 * width * width), F32),
            jax.ShapeDtypeStruct((2, n_dp, per_dp, group, width), BF16),
        ),
        in_specs=[any_space, vmem, vmem, vmem, vmem, any_space, any_space],
        out_specs=(vmem, any_space),
        scratch_shapes=[
            pltpu.VMEM((local_images, nodes, samples), BF16),
            pltpu.VMEM((slots, nodes, width), BF16),
            pltpu.VMEM((slots, width, width), BF16),
            pltpu.VMEM((2 * slot_total, samples), BF16),
            pltpu.VMEM((slots, nodes, width), BF16),
            pltpu.VMEM((chip_rows * local_images, nodes), F32),
            pltpu.VMEM((n_peers, per_dp, block, nodes), BF16),
            pltpu.VMEM((per_dp, n_order, block, nodes), BF16),
            pltpu.VMEM((per_dp, 2, n_dp, group, width), BF16),
            pltpu.VMEM((per_dp, 2, half, width, width), BF16),
            pltpu.VMEM((per_dp, half, width, width), BF16),
            pltpu.VMEM((per_dp, half, width, width), BF16),
            pltpu.VMEM((per_dp, half, width, width), BF16),
            pltpu.VMEM((2 * width * per_dp, width), F32),
            dma((parts,)),
            dma((2,)),
            dma((n_peers, per_dp)),
            dma((n_peers, per_dp)),
            dma((per_dp,)),
            dma((per_dp,)),
            dma((per_dp, half)),
            dma((per_dp, half)),
            dma((per_dp,)),
        ],
        compiler_params=pltpu.CompilerParams(
            collective_id=0, has_side_effects=True, vmem_limit_bytes=60 * 2**20
        ),
        cost_estimate=pl.CostEstimate(
            flops=5_000_000_000, bytes_accessed=14_000_000, transcendentals=0
        ),
    )(images, radial_interp, row_index, base, mask, radial_basis, eigenbasis)
    return covariance, projected.reshape(2, slots, group, width)


def solution(mesh):
    placed = (
        P(("dp", "order"), None, None),
        P(),
        P(),
        P("order"),
        P("order", None, None),
        P("order", None, None),
    )
    return jax.shard_map(
        functools.partial(body, mesh.shape["order"], mesh.shape["dp"]),
        mesh=mesh,
        in_specs=placed,
        out_specs=(P(("order", "dp"), None), P(None, "order", "dp", None)),
        check_vma=False,
    )
```

profile of v0, /device:TPU:0, one launch (start us, length us, event | category | flops | bytes accessed | tf_op | source)
XLA Modules:
  0.0 83.4 jit_solution(6647979887066431199)
XLA Ops:
  0.6 0.8 reshape.69
  1.4 0.1 copy.9
  1.5 1.4 %compare_convert_fusion.mask = f32[64,1,128]{2,1,0:T(1,128)} fusion(s32[64]{0:T(128)} %param.10), kind=kLoop, calls=%fused_computation | loop fusion | flops 16384 | bytes 33024 | tf_op jit(solution)/shard_map/convert_element_type | solution.py:245
  2.9 0.1 broadcast_add_fusion
  3.0 0.8 add.27.row_index
  3.8 72.5 %shard_map.86 = (f32[8,32768]{1,0:T(8,128)}, bf16[2,8,8,128,128]{4,3,2,1,0:T(8,128)(2,1)}) custom-call(bf16[32,128,512]{2,1,0:T(8,128)(2,1)} %images_hbm.1, bf16[128,128]{1,0:T(8,128)(2,1)} %interp.1, s32[512,1]{1,0:T(8,128)} %add.27.row_index, bf16[512,512]{1,0:T(8,128)(2,1)} %constant.4.clone.base, f32[64,1,128]{2,1,0:T(1,128)} %compare_convert_fusion.mask, ...), custom_call_target="tpu_custom_call" | custom-call | flops 5000000000 | bytes 14000000 | tf_op jit(solution)/shard_map/pallas_call | solution.py:256
  76.3 2.3 %copy.13 = f32[8,32768]{1,0:T(8,128)} copy(f32[8,32768]{1,0:T(8,128)} %get-tuple-element.8) | data formatting | bytes 2097152
  78.6 4.8 %copy.14 = bf16[2,64,128,128]{3,2,1,0:T(8,128)(2,1)} copy(bf16[2,64,128,128]{3,2,1,0:T(8,128)(2,1)} %bitcast.4) | data formatting | bytes 8388608
  (1 shorter events, 0.0 us)
where the time goes:
time: 83.6 us; the launch traced here: 83.4 us
  Pallas kernels  72.5 us (87%)
  local copies, waits for them, and re-layouts  8.69 us (10%)
  other arithmetic  1.51 us (2%)
    pallas_call x1, Pallas kernels, body(): pl.pallas_call(functools.partial(kernel, n_order, n_dp), out_shape=(jax.S...  72.5 us
    unnamed x2, local copies, waits for them, and re-layouts  7.05 us

commit v1 on v0

--- a/solution.py
+++ b/solution.py
@@ -14,7 +14,7 @@
 BF16 = jnp.bfloat16
 F32 = jnp.float32
 CORES = 2
-WINDOW = 4
+WINDOW = 2
 
 
 def base_table(orders, samples):
@@ -25,16 +25,16 @@
 
 
 def kernel(
-    n_order, n_dp, images_hbm, interp, row_index, base, mask, basis_hbm, eigen_hbm,
+    n_order, n_dp, images_hbm, interp_hbm, assignment, base_hbm, counts, basis_hbm, eigen_hbm,
     cov_out, proj_out,
-    images, basis, eigen, table, kept, wide, send, recv, proj, cov_own, cov_y, cov_z, cov_got,
-    cov_rows, image_sem, weight_sem, spec_send, spec_recv, y_send, y_recv, z_send, z_recv, proj_sem,
+    interp, base, images, basis, eigen, table, kept, wide, send, recv, proj, cov_own, cov_y, cov_z, cov_got,
+    image_sem, weight_sem, spec_send, spec_recv, y_send, y_recv, z_send, z_recv, proj_sem,
 ):
     local_images, nodes, samples = images.shape
     slots = basis.shape[0]
     chips, half, per_dp = n_order // CORES, n_dp // 2, slots // n_dp
     chip_rows = CORES * slots * 2
-    block = 2 * n_dp * local_images
+    block = n_dp * local_images
     me, my_dp = lax.axis_index("order"), lax.axis_index("dp")
     my_chip, my_core = me // CORES, me % CORES
     my_z, my_y = my_dp // 2, my_dp % 2
@@ -67,24 +67,40 @@
         )
         for n in range(parts)
     ]
+    base_copy = pltpu.make_async_copy(base_hbm, base, weight_sem.at[2])
+    interp_copy = pltpu.make_async_copy(interp_hbm, interp, weight_sem.at[3])
+    base_copy.start()
     for copy in image_copies:
         copy.start()
+    interp_copy.start()
     basis_copy = pltpu.make_async_copy(basis_hbm, basis, weight_sem.at[0])
     eigen_copy = pltpu.make_async_copy(eigen_hbm, eigen, weight_sem.at[1])
     basis_copy.start()
     eigen_copy.start()
 
-    total_rows = table.shape[0]
-    for r in range(0, total_rows, 128):
-        hot = row_index[pl.ds(r, 128), :] == lax.broadcasted_iota(
-            jnp.int32, (128, base.shape[0]), 1
-        )
-        table[pl.ds(r, 128), :] = jnp.dot(
-            hot.astype(F32).astype(BF16), base[...], preferred_element_type=F32
+    total = n_order * slots
+    row = lax.broadcasted_iota(jnp.int32, (total, total), 0)
+    lane = lax.broadcasted_iota(jnp.int32, (total, total), 1)
+    owner, chunk, dp_owner = lane // slots, (lane % slots) // n_dp, lane % n_dp
+    to_row = row == owner * slots + dp_owner * per_dp + chunk
+    is_order = row == assignment[...]
+    pick = jnp.dot(
+        is_order.astype(F32).astype(BF16),
+        to_row.astype(F32).astype(BF16),
+        preferred_element_type=F32,
+    ).astype(BF16)
+    base_copy.wait()
+    for p in range(2):
+        table[p] = lax.dot_general(
+            pick, base[pl.ds(p * total, total), :],
+            (((0,), (0,)), ((), ())), preferred_element_type=F32,
         ).astype(BF16)
 
     def transform(dx, first):
-        start = pl.multiple_of(lax.rem(my_chip + dx, chips) * chip_rows, chip_rows)
+        start = pl.multiple_of(
+            lax.rem(my_chip + dx, chips) * (chip_rows // 2), chip_rows // 2
+        )
+        rows = table[:, pl.ds(start, chip_rows // 2), :].reshape(chip_rows, samples)
         for n in range(parts):
             if first:
                 image_copies[n].wait()
@@ -94,7 +110,7 @@
                 i = n * per_part + h * 2
                 pair = images[pl.ds(i, 2)].reshape(2 * nodes, samples)
                 got = lax.dot_general(
-                    table[pl.ds(start, chip_rows), :], pair,
+                    rows, pair,
                     (((1,), (1,)), ((), ())), preferred_element_type=F32,
                 )
                 wide[pl.ds(i, chip_rows, stride=local_images), :] = got[:, :nodes]
@@ -111,10 +127,10 @@
             device_id_type=MESH,
         )
 
-    def rows_of(dc, k):
-        return pl.ds(
-            pl.multiple_of((lax.rem(my_core + dc, CORES) * per_dp + k) * block, block), block
-        )
+    def narrowed(dc, k, p):
+        core = lax.rem(my_core + dc, CORES)
+        at = pl.multiple_of(((p * CORES + core) * per_dp + k) * block, block)
+        return wide[pl.ds(at, block), :].astype(BF16)
 
     far = len(peers) - 1
     for dx in range(1, chips):
@@ -124,23 +140,27 @@
         for k in range(per_dp):
             for dc in range(CORES):
                 t = (dx - 1) * CORES + dc
-                send[t, k] = wide[rows_of(dc, k), :].astype(BF16)
+                for p in range(2):
+                    send[t, k, p] = narrowed(dc, k, p)
                 if k < WINDOW:
                     spec_copy(k, t).start()
     transform(0, chips == 1)
     for k in range(per_dp):
-        send[far, k] = wide[rows_of(1, k), :].astype(BF16)
+        for p in range(2):
+            send[far, k, p] = narrowed(1, k, p)
         spec_copy(k, far).start()
     for k in range(per_dp):
-        recv[k, me] = wide[rows_of(0, k), :].astype(BF16)
+        for p in range(2):
+            recv[k, me, p] = narrowed(0, k, p)
 
     basis_copy.wait()
+    interp_copy.wait()
+    column = lax.broadcasted_iota(jnp.int32, (1, kept.shape[2]), 1)
 
     @pl.loop(0, slots)
     def _(j):
-        kept[j] = (
-            jnp.dot(interp[...], basis[j], preferred_element_type=F32) * mask[j]
-        ).astype(BF16)
+        folded = jnp.dot(interp[...], basis[j], preferred_element_type=F32)
+        kept[j] = jnp.where(column < counts[j], folded, 0.0).astype(BF16)
 
     eigen_copy.wait()
     scale = 1.0 / (local_images * n_order * n_dp)
@@ -174,11 +194,16 @@
             for y in range(2):
                 d = z * 2 + y
                 j = d * per_dp + k
-                at = pl.multiple_of(d * 2 * local_images, 2 * local_images)
-                got = recv[k, :, pl.ds(at, 2 * local_images), :]
+                at = pl.multiple_of(d * local_images, local_images)
                 both = jnp.concatenate(
-                    [got[:, :local_images], got[:, local_images:]], 0
-                ).reshape(2 * n_order * local_images, nodes)
+                    [
+                        recv[k, :, p, pl.ds(at, local_images), :].reshape(
+                            n_order * local_images, nodes
+                        )
+                        for p in range(2)
+                    ],
+                    0,
+                )
                 coef = jnp.dot(both, kept[j], preferred_element_type=F32).astype(BF16)
                 real, imag = coef[: n_order * local_images], coef[n_order * local_images :]
                 mixed = jnp.concatenate([real - imag, real + imag], 0)
@@ -201,17 +226,14 @@
         for q in range(1, half):
             z_copy(k, q).wait_recv()
             whole = whole + cov_got[k, q].astype(F32)
-        flipped = whole.T
-        width = whole.shape[0]
-        cov_rows[pl.ds(k, width, stride=per_dp), :] = (whole + flipped) * 0.5
-        cov_rows[pl.ds(width * per_dp + k, width, stride=per_dp), :] = (whole - flipped) * 0.5
+        cov_out[k] = whole
 
     for k in range(per_dp):
+        for t in range(len(peers)):
+            spec_copy(k, t).wait_recv()
         if k + WINDOW < per_dp:
             for t in range(far):
                 spec_copy(k + WINDOW, t).start()
-        for t in range(len(peers)):
-            spec_copy(k, t).wait_recv()
         slot_work(k)
         y_copy(k).start()
         proj_copy(k).start()
@@ -222,8 +244,6 @@
     reduce_y(per_dp - 1)
     for k in range(max(0, per_dp - 2), per_dp):
         reduce_z(k)
-    for r in range(cov_rows.shape[0] // per_dp):
-        cov_out[:, pl.ds(r * 128, 128)] = cov_rows[pl.ds(r * per_dp, per_dp), :]
     for k in range(per_dp):
         for t in range(len(peers)):
             spec_copy(k, t).wait_send()
@@ -233,51 +253,73 @@
         proj_copy(k).wait()
 
 
+def finish(whole, proj, cov_out, proj_out, rows, sems):
+    parts = [(p, z) for p in range(2) for z in range(sems.shape[1])]
+    size = proj.shape[1] // sems.shape[1]
+    copies = [
+        pltpu.make_async_copy(
+            proj.at[p, pl.ds(z * size, size)], proj_out.at[p, pl.ds(z * size, size)], sems.at[p, z]
+        )
+        for p, z in parts
+    ]
+    for copy in copies:
+        copy.start()
+    slots, width, _ = whole.shape
+    for k in range(slots):
+        one = whole[k]
+        flipped = one.T
+        rows[pl.ds(k, width, stride=slots), :] = (one + flipped) * 0.5
+        rows[pl.ds(width * slots + k, width, stride=slots), :] = (one - flipped) * 0.5
+    for r in range(2 * width):
+        cov_out[:, pl.ds(r * width, width)] = rows[pl.ds(r * slots, slots), :]
+    for copy in copies:
+        copy.wait()
+
+
 def body(n_order, n_dp, images, radial_interp, assignment, counts, radial_basis, eigenbasis):
     local_images, nodes, samples = images.shape
     slot_total = assignment.shape[0]
     slots, _, width = radial_basis.shape
     per_dp, half, chips = slots // n_dp, n_dp // 2, n_order // CORES
-    placed = assignment.reshape(n_order, n_dp, per_dp).transpose(0, 2, 1)
-    row_index = (
-        placed[..., None] + slot_total * jnp.arange(2, dtype=jnp.int32)
-    ).reshape(2 * slot_total, 1)
-    mask = (jnp.arange(width, dtype=jnp.int32)[None, :] < counts[:, None]).astype(F32)
-    mask = mask.reshape(slots, 1, width)
     base = jnp.asarray(base_table(slot_total, samples))
-    block = 2 * n_dp * local_images
+    block = n_dp * local_images
     n_peers = n_order - 1
     chip_rows = CORES * slots * 2
     parts = 4
     vmem = pl.BlockSpec(memory_space=pltpu.VMEM)
     any_space = pl.BlockSpec(memory_space=pl.ANY)
+    hbm = pl.BlockSpec(memory_space=pltpu.HBM)
     dma = pltpu.SemaphoreType.DMA
     group = n_order * local_images
-    covariance, projected = pl.pallas_call(
+    whole, projected = pl.pallas_call(
         functools.partial(kernel, n_order, n_dp),
         out_shape=(
-            jax.ShapeDtypeStruct((per_dp, 2 * width * width), F32),
+            jax.ShapeDtypeStruct((per_dp, width, width), F32),
             jax.ShapeDtypeStruct((2, n_dp, per_dp, group, width), BF16),
         ),
-        in_specs=[any_space, vmem, vmem, vmem, vmem, any_space, any_space],
+        in_specs=[
+            hbm, hbm, vmem, hbm, pl.BlockSpec(memory_space=pltpu.SMEM),
+            hbm, hbm,
+        ],
         out_specs=(vmem, any_space),
         scratch_shapes=[
+            pltpu.VMEM((nodes, nodes), BF16),
+            pltpu.VMEM((2 * slot_total, samples), BF16),
             pltpu.VMEM((local_images, nodes, samples), BF16),
             pltpu.VMEM((slots, nodes, width), BF16),
             pltpu.VMEM((slots, width, width), BF16),
-            pltpu.VMEM((2 * slot_total, samples), BF16),
+            pltpu.VMEM((2, slot_total, samples), BF16),
             pltpu.VMEM((slots, nodes, width), BF16),
             pltpu.VMEM((chip_rows * local_images, nodes), F32),
-            pltpu.VMEM((n_peers, per_dp, block, nodes), BF16),
-            pltpu.VMEM((per_dp, n_order, block, nodes), BF16),
+            pltpu.VMEM((n_peers, per_dp, 2, block, nodes), BF16),
+            pltpu.VMEM((per_dp, n_order, 2, block, nodes), BF16),
             pltpu.VMEM((per_dp, 2, n_dp, group, width), BF16),
             pltpu.VMEM((per_dp, 2, half, width, width), BF16),
             pltpu.VMEM((per_dp, half, width, width), BF16),
             pltpu.VMEM((per_dp, half, width, width), BF16),
             pltpu.VMEM((per_dp, half, width, width), BF16),
-            pltpu.VMEM((2 * width * per_dp, width), F32),
             dma((parts,)),
-            dma((2,)),
+            dma((4,)),
             dma((n_peers, per_dp)),
             dma((n_peers, per_dp)),
             dma((per_dp,)),
@@ -287,13 +329,27 @@
             dma((per_dp,)),
         ],
         compiler_params=pltpu.CompilerParams(
-            collective_id=0, has_side_effects=True, vmem_limit_bytes=60 * 2**20
+            collective_id=0, has_side_effects=True, vmem_limit_bytes=44 * 2**20
         ),
         cost_estimate=pl.CostEstimate(
             flops=5_000_000_000, bytes_accessed=14_000_000, transcendentals=0
         ),
-    )(images, radial_interp, row_index, base, mask, radial_basis, eigenbasis)
-    return covariance, projected.reshape(2, slots, group, width)
+    )(images, radial_interp, assignment.reshape(1, -1), base, counts, radial_basis, eigenbasis)
+    projected = projected.reshape(2, slots, group, width)
+    return pl.pallas_call(
+        finish,
+        out_shape=(
+            jax.ShapeDtypeStruct((per_dp, 2 * width * width), F32),
+            jax.ShapeDtypeStruct(projected.shape, BF16),
+        ),
+        in_specs=[vmem, any_space],
+        out_specs=(vmem, any_space),
+        scratch_shapes=[pltpu.VMEM((2 * width * per_dp, width), F32), dma((2, 4))],
+        compiler_params=pltpu.CompilerParams(vmem_limit_bytes=16 * 2**20),
+        cost_estimate=pl.CostEstimate(
+            flops=1_000_000, bytes_accessed=10_000_000, transcendentals=0
+        ),
+    )(whole, projected)
 
 
 def solution(mesh):

time: 83.6 us -> 85.5 us (1.023)
  Pallas kernels: 72.5 us -> 78.3 us
  local copies, waits for them, and re-layouts: 8.69 us -> 6.31 us
  other arithmetic: 1.51 us -> 0 us
    pallas_call x0 -> x1, Pallas kernels: none -> 3.05 us  [body(): pl.pallas_call(finish, out_shape=(jax.ShapeDtypeStruct((per_dp, 2 * width...]
    pallas_call x1, Pallas kernels: 72.5 us -> 75.2 us  [body(): pl.pallas_call(functools.partial(kernel, n_order, n_dp), out_shape=(jax.S...]
    convert_element_type x1 -> x0, other arithmetic: 1.42 us -> none  [body(): (jnp.arange(width, dtype=jnp.int32)[None, :] < counts[:, None]).astype(F32)]
    unnamed x2 -> x12, local copies, waits for them, and re-layouts: 7.05 us -> 6.31 us
where the time goes in v1:
time: 85.5 us; the launch traced here: 85.2 us
  Pallas kernels  78.3 us (92%)
  local copies, waits for them, and re-layouts  6.31 us (7%)
    pallas_call x1, Pallas kernels, body(): pl.pallas_call(functools.partial(kernel, n_order, n_dp), out_shape=(jax.S...  75.2 us
    unnamed x12, local copies, waits for them, and re-layouts  6.31 us
    pallas_call x1, Pallas kernels, body(): pl.pallas_call(finish, out_shape=(jax.ShapeDtypeStruct((per_dp, 2 * width...  3.05 us

profile of v1, /device:TPU:0, one launch (start us, length us, event | category | flops | bytes accessed | tf_op | source)
XLA Modules:
  0.0 85.2 jit_solution(16615092398245672856)
XLA Ops:
  0.6 0.0 copy-start
  0.6 1.6 %copy-done = bf16[64,128,128]{2,1,0:T(8,128)(2,1)S(1)} copy-done((bf16[64,128,128]{2,1,0:T(8,128)(2,1)S(1)}, bf16[64,128,128]{2,1,0:T(8,128)(2,1)}, u32[]{:S(2)}) %copy-start) | copy-done | bytes 2097176
  2.2 0.0 copy-start.1
  2.2 1.6 %copy-done.1 = bf16[64,128,128]{2,1,0:T(8,128)(2,1)S(1)} copy-done((bf16[64,128,128]{2,1,0:T(8,128)(2,1)S(1)}, bf16[64,128,128]{2,1,0:T(8,128)(2,1)}, u32[]{:S(2)}) %copy-start.1) | copy-done | bytes 2097176
  3.8 0.0 copy-start.2
  3.8 0.8 copy-done.2
  4.6 0.0 copy-start.3
  4.6 0.7 copy-done.3
  5.3 0.0 copy-start.4
  5.3 0.7 copy-done.4
  5.9 0.0 copy-start.5
  5.9 1.0 %copy-done.5 = bf16[512,512]{1,0:T(8,128)(2,1)S(1)} copy-done((bf16[512,512]{1,0:T(8,128)(2,1)S(1)}, bf16[512,512]{1,0:T(8,128)(2,1)}, u32[]{:S(2)}) %copy-start.5) | copy-done | bytes 524312
  7.0 75.2 %shard_map.86 = (f32[8,128,128]{2,1,0:T(8,128)S(1)}, bf16[2,8,8,128,128]{4,3,2,1,0:T(8,128)(2,1)S(1)}) custom-call(bf16[32,128,512]{2,1,0:T(8,128)(2,1)} %images_hbm.1, bf16[128,128]{1,0:T(8,128)(2,1)S(1)} %copy-done.2, s32[1,256]{1,0:T(1,128)S(1)} %bitcast.3, bf16[512,512]{1,0:T(8,128)(2,1)S(1)} %copy-done.5, s32[64]{0:T(128)S(1)} %copy-done.4, ...), custom_call_target="tpu_custom_call" | custom-call | flops 5000000000 | bytes 14000000 | tf_op jit(solution)/shard_map/pallas_call | solution.py:294
  82.2 3.1 %shard_map.87 = (f32[8,32768]{1,0:T(8,128)}, bf16[2,64,128,128]{3,2,1,0:T(8,128)(2,1)}) custom-call(f32[8,128,128]{2,1,0:T(8,128)S(1)} %get-tuple-element.4.whole, bf16[2,64,128,128]{3,2,1,0:T(8,128)(2,1)S(1)} %bitcast.2), custom_call_target="tpu_custom_call" | custom-call | flops 1000000 | bytes 10000000 | tf_op jit(solution)/shard_map/pallas_call | solution.py:339
Async XLA Ops:
  0.6 1.6 %copy-start = (bf16[64,128,128]{2,1,0:T(8,128)(2,1)S(1)}, bf16[64,128,128]{2,1,0:T(8,128)(2,1)}, u32[]{:S(2)}) copy-start(bf16[64,128,128]{2,1,0:T(8,128)(2,1)} %basis_hbm.1) | copy-start | bytes 6291460
  2.2 1.6 %copy-start.1 = (bf16[64,128,128]{2,1,0:T(8,128)(2,1)S(1)}, bf16[64,128,128]{2,1,0:T(8,128)(2,1)}, u32[]{:S(2)}) copy-start(bf16[64,128,128]{2,1,0:T(8,128)(2,1)} %eigen_hbm.1) | copy-start | bytes 6291460
  3.8 0.8 copy-start.2
  4.6 0.7 copy-start.3
  5.3 0.7 copy-start.4
  5.9 1.0 %copy-start.5 = (bf16[512,512]{1,0:T(8,128)(2,1)S(1)}, bf16[512,512]{1,0:T(8,128)(2,1)}, u32[]{:S(2)}) copy-start(bf16[512,512]{1,0:T(8,128)(2,1)} %constant.2.clone.base_hbm) | copy-start | bytes 1572868

commit v2 on v1

--- a/solution.py
+++ b/solution.py
@@ -14,7 +14,7 @@
 BF16 = jnp.bfloat16
 F32 = jnp.float32
 CORES = 2
-WINDOW = 2
+WINDOW = 8
 
 
 def base_table(orders, samples):
@@ -25,9 +25,9 @@
 
 
 def kernel(
-    n_order, n_dp, images_hbm, interp_hbm, assignment, base_hbm, counts, basis_hbm, eigen_hbm,
+    n_order, n_dp, images_hbm, interp_hbm, assignment_hbm, base_hbm, counts_hbm, basis_hbm, eigen_hbm,
     cov_out, proj_out,
-    interp, base, images, basis, eigen, table, kept, wide, send, recv, proj, cov_own, cov_y, cov_z, cov_got,
+    assignment, counts, interp, base, images, basis, eigen, table, kept, wide, send, recv, proj, cov_own, cov_y, cov_z, cov_got,
     image_sem, weight_sem, spec_send, spec_recv, y_send, y_recv, z_send, z_recv, proj_sem,
 ):
     local_images, nodes, samples = images.shape
@@ -69,6 +69,10 @@
     ]
     base_copy = pltpu.make_async_copy(base_hbm, base, weight_sem.at[2])
     interp_copy = pltpu.make_async_copy(interp_hbm, interp, weight_sem.at[3])
+    assignment_copy = pltpu.make_async_copy(assignment_hbm, assignment, weight_sem.at[4])
+    counts_copy = pltpu.make_async_copy(counts_hbm, counts, weight_sem.at[5])
+    assignment_copy.start()
+    counts_copy.start()
     base_copy.start()
     for copy in image_copies:
         copy.start()
@@ -83,6 +87,7 @@
     lane = lax.broadcasted_iota(jnp.int32, (total, total), 1)
     owner, chunk, dp_owner = lane // slots, (lane % slots) // n_dp, lane % n_dp
     to_row = row == owner * slots + dp_owner * per_dp + chunk
+    assignment_copy.wait()
     is_order = row == assignment[...]
     pick = jnp.dot(
         is_order.astype(F32).astype(BF16),
@@ -155,6 +160,7 @@
 
     basis_copy.wait()
     interp_copy.wait()
+    counts_copy.wait()
     column = lax.broadcasted_iota(jnp.int32, (1, kept.shape[2]), 1)
 
     @pl.loop(0, slots)
@@ -286,6 +292,7 @@
     n_peers = n_order - 1
     chip_rows = CORES * slots * 2
     parts = 4
+    in_hbm = functools.partial(pltpu.with_memory_space_constraint, memory_space=pltpu.HBM)
     vmem = pl.BlockSpec(memory_space=pltpu.VMEM)
     any_space = pl.BlockSpec(memory_space=pl.ANY)
     hbm = pl.BlockSpec(memory_space=pltpu.HBM)
@@ -297,12 +304,11 @@
             jax.ShapeDtypeStruct((per_dp, width, width), F32),
             jax.ShapeDtypeStruct((2, n_dp, per_dp, group, width), BF16),
         ),
-        in_specs=[
-            hbm, hbm, vmem, hbm, pl.BlockSpec(memory_space=pltpu.SMEM),
-            hbm, hbm,
-        ],
+        in_specs=[hbm] * 7,
         out_specs=(vmem, any_space),
         scratch_shapes=[
+            pltpu.VMEM((1, slot_total), jnp.int32),
+            pltpu.SMEM((slots,), jnp.int32),
             pltpu.VMEM((nodes, nodes), BF16),
             pltpu.VMEM((2 * slot_total, samples), BF16),
             pltpu.VMEM((local_images, nodes, samples), BF16),
@@ -319,7 +325,7 @@
             pltpu.VMEM((per_dp, half, width, width), BF16),
             pltpu.VMEM((per_dp, half, width, width), BF16),
             dma((parts,)),
-            dma((4,)),
+            dma((6,)),
             dma((n_peers, per_dp)),
             dma((n_peers, per_dp)),
             dma((per_dp,)),
@@ -334,7 +340,15 @@
         cost_estimate=pl.CostEstimate(
             flops=5_000_000_000, bytes_accessed=14_000_000, transcendentals=0
         ),
-    )(images, radial_interp, assignment.reshape(1, -1), base, counts, radial_basis, eigenbasis)
+    )(
+        *map(
+            in_hbm,
+            (
+                images, radial_interp, assignment.reshape(1, -1), base, counts,
+                radial_basis, eigenbasis,
+            ),
+        )
+    )
     projected = projected.reshape(2, slots, group, width)
     return pl.pallas_call(
         finish,

time: 85.5 us -> 74.4 us (0.87)
  local copies, waits for them, and re-layouts: 6.31 us -> 0 us
  Pallas kernels: 78.3 us -> 73.6 us
    unnamed x12 -> x0, local copies, waits for them, and re-layouts: 6.31 us -> none
    pallas_call x1, Pallas kernels: 75.2 us -> 70.6 us  [body(): pl.pallas_call(functools.partial(kernel, n_order, n_dp), out_shape=(jax.S...]
where the time goes in v2:
time: 74.4 us; the launch traced here: 74.3 us
  Pallas kernels  73.6 us (99%)
    pallas_call x1, Pallas kernels, body(): pl.pallas_call(functools.partial(kernel, n_order, n_dp), out_shape=(jax.S...  70.6 us
    pallas_call x1, Pallas kernels, body(): pl.pallas_call(finish, out_shape=(jax.ShapeDtypeStruct((per_dp, 2 * width...  3.05 us

profile of v2, /device:TPU:0, one launch (start us, length us, event | category | flops | bytes accessed | tf_op | source)
XLA Modules:
  0.0 74.3 jit_solution(7638084485080814358)
XLA Ops:
  0.6 70.6 %shard_map.86 = (f32[8,128,128]{2,1,0:T(8,128)S(1)}, bf16[2,8,8,128,128]{4,3,2,1,0:T(8,128)(2,1)S(1)}) custom-call(bf16[32,128,512]{2,1,0:T(8,128)(2,1)} %images_hbm.1, bf16[128,128]{1,0:T(8,128)(2,1)} %interp_hbm.1, s32[1,256]{1,0:T(1,128)} %bitcast.3, bf16[512,512]{1,0:T(8,128)(2,1)} %constant.2.clone.base_hbm, s32[64]{0:T(128)} %counts_hbm.1, ...), custom_call_target="tpu_custom_call" | custom-call | flops 5000000000 | bytes 14000000 | tf_op jit(solution)/shard_map/pallas_call | solution.py:301
  71.2 3.1 %shard_map.87 = (f32[8,32768]{1,0:T(8,128)}, bf16[2,64,128,128]{3,2,1,0:T(8,128)(2,1)}) custom-call(f32[8,128,128]{2,1,0:T(8,128)S(1)} %get-tuple-element.4.whole, bf16[2,64,128,128]{3,2,1,0:T(8,128)(2,1)S(1)} %bitcast.2), custom_call_target="tpu_custom_call" | custom-call | flops 1000000 | bytes 10000000 | tf_op jit(solution)/shard_map/pallas_call | solution.py:353

commit v3 on v2

--- a/solution.py
+++ b/solution.py
@@ -14,7 +14,6 @@
 BF16 = jnp.bfloat16
 F32 = jnp.float32
 CORES = 2
-WINDOW = 8
 
 
 def base_table(orders, samples):
@@ -85,8 +84,10 @@
     total = n_order * slots
     row = lax.broadcasted_iota(jnp.int32, (total, total), 0)
     lane = lax.broadcasted_iota(jnp.int32, (total, total), 1)
-    owner, chunk, dp_owner = lane // slots, (lane % slots) // n_dp, lane % n_dp
-    to_row = row == owner * slots + dp_owner * per_dp + chunk
+    step = n_dp * CORES
+    chip, chunk = lane // (step * per_dp), (lane // step) % per_dp
+    core, dp_owner = (lane // n_dp) % CORES, lane % n_dp
+    to_row = row == (chip * CORES + core) * slots + dp_owner * per_dp + chunk
     assignment_copy.wait()
     is_order = row == assignment[...]
     pick = jnp.dot(
@@ -101,11 +102,10 @@
             (((0,), (0,)), ((), ())), preferred_element_type=F32,
         ).astype(BF16)
 
-    def transform(dx, first):
-        start = pl.multiple_of(
-            lax.rem(my_chip + dx, chips) * (chip_rows // 2), chip_rows // 2
-        )
-        rows = table[:, pl.ds(start, chip_rows // 2), :].reshape(chip_rows, samples)
+    def transform(dx, k0, k1, first):
+        at = lax.rem(my_chip + dx, chips) * (step * per_dp) + k0 * step
+        count = (k1 - k0) * step
+        rows = table[:, pl.ds(pl.multiple_of(at, step), count), :].reshape(2 * count, samples)
         for n in range(parts):
             if first:
                 image_copies[n].wait()
@@ -118,8 +118,8 @@
                     rows, pair,
                     (((1,), (1,)), ((), ())), preferred_element_type=F32,
                 )
-                wide[pl.ds(i, chip_rows, stride=local_images), :] = got[:, :nodes]
-                wide[pl.ds(i + 1, chip_rows, stride=local_images), :] = got[:, nodes:]
+                wide[pl.ds(i, 2 * count, stride=local_images), :] = got[:, :nodes]
+                wide[pl.ds(i + 1, 2 * count, stride=local_images), :] = got[:, nodes:]
 
     def spec_copy(k, t):
         dx, dc = peers[t]
@@ -132,31 +132,32 @@
             device_id_type=MESH,
         )
 
-    def narrowed(dc, k, p):
+    def narrowed(dc, k, k0, k1, p):
         core = lax.rem(my_core + dc, CORES)
-        at = pl.multiple_of(((p * CORES + core) * per_dp + k) * block, block)
+        at = pl.multiple_of(((p * (k1 - k0) + k - k0) * CORES + core) * block, block)
         return wide[pl.ds(at, block), :].astype(BF16)
 
     far = len(peers) - 1
+    groups = [(0, 2), (2, per_dp)] if per_dp > 2 else [(0, per_dp)]
     for dx in range(1, chips):
-        transform(dx, dx == 1)
-        if dx == 1:
-            pl.semaphore_wait(barrier, len(peers) + half)
-        for k in range(per_dp):
-            for dc in range(CORES):
-                t = (dx - 1) * CORES + dc
-                for p in range(2):
-                    send[t, k, p] = narrowed(dc, k, p)
-                if k < WINDOW:
+        for k0, k1 in groups:
+            transform(dx, k0, k1, dx == 1 and k0 == 0)
+            if dx == 1 and k0 == 0:
+                pl.semaphore_wait(barrier, len(peers) + half)
+            for k in range(k0, k1):
+                for dc in range(CORES):
+                    t = (dx - 1) * CORES + dc
+                    for p in range(2):
+                        send[t, k, p] = narrowed(dc, k, k0, k1, p)
                     spec_copy(k, t).start()
-    transform(0, chips == 1)
+    transform(0, 0, per_dp, chips == 1)
     for k in range(per_dp):
         for p in range(2):
-            send[far, k, p] = narrowed(1, k, p)
+            send[far, k, p] = narrowed(1, k, 0, per_dp, p)
         spec_copy(k, far).start()
     for k in range(per_dp):
         for p in range(2):
-            recv[k, me, p] = narrowed(0, k, p)
+            recv[k, me, p] = narrowed(0, k, 0, per_dp, p)
 
     basis_copy.wait()
     interp_copy.wait()
@@ -194,10 +195,10 @@
     def proj_copy(k):
         return pltpu.make_async_copy(proj.at[k], proj_out.at[:, :, k], proj_sem.at[k])
 
-    def slot_work(k):
-        @pl.loop(0, half)
-        def _(z):
-            for y in range(2):
+    def slot_work(k, y):
+        @pl.loop(0, half // 2)
+        def _(h):
+            for z in (h * 2, h * 2 + 1):
                 d = z * 2 + y
                 j = d * per_dp + k
                 at = pl.multiple_of(d * local_images, local_images)
@@ -237,11 +238,9 @@
     for k in range(per_dp):
         for t in range(len(peers)):
             spec_copy(k, t).wait_recv()
-        if k + WINDOW < per_dp:
-            for t in range(far):
-                spec_copy(k + WINDOW, t).start()
-        slot_work(k)
+        slot_work(k, 1 - my_y)
         y_copy(k).start()
+        slot_work(k, my_y)
         proj_copy(k).start()
         if k >= 1:
             reduce_y(k - 1)

time: 74.4 us -> 71 us (0.954)
  Pallas kernels: 73.6 us -> 70.2 us
    pallas_call x1, Pallas kernels: 70.6 us -> 67.1 us  [body(): pl.pallas_call(functools.partial(kernel, n_order, n_dp), out_shape=(jax.S...]
where the time goes in v3:
time: 71 us; the launch traced here: 70.8 us
  Pallas kernels  70.2 us (99%)
    pallas_call x1, Pallas kernels, body(): pl.pallas_call(functools.partial(kernel, n_order, n_dp), out_shape=(jax.S...  67.1 us
    pallas_call x1, Pallas kernels, body(): pl.pallas_call(finish, out_shape=(jax.ShapeDtypeStruct((per_dp, 2 * width...  3.05 us

profile of v3, /device:TPU:0, one launch (start us, length us, event | category | flops | bytes accessed | tf_op | source)
XLA Modules:
  0.0 70.8 jit_solution(15729488529198851408)
XLA Ops:
  0.6 67.1 %shard_map.86 = (f32[8,128,128]{2,1,0:T(8,128)S(1)}, bf16[2,8,8,128,128]{4,3,2,1,0:T(8,128)(2,1)S(1)}) custom-call(bf16[32,128,512]{2,1,0:T(8,128)(2,1)} %images_hbm.1, bf16[128,128]{1,0:T(8,128)(2,1)} %interp_hbm.1, s32[1,256]{1,0:T(1,128)} %bitcast.3, bf16[512,512]{1,0:T(8,128)(2,1)} %constant.2.clone.base_hbm, s32[64]{0:T(128)} %counts_hbm.1, ...), custom_call_target="tpu_custom_call" | custom-call | flops 5000000000 | bytes 14000000 | tf_op jit(solution)/shard_map/pallas_call | solution.py:300
  67.7 3.1 %shard_map.87 = (f32[8,32768]{1,0:T(8,128)}, bf16[2,64,128,128]{3,2,1,0:T(8,128)(2,1)}) custom-call(f32[8,128,128]{2,1,0:T(8,128)S(1)} %get-tuple-element.4.whole, bf16[2,64,128,128]{3,2,1,0:T(8,128)(2,1)S(1)} %bitcast.2), custom_call_target="tpu_custom_call" | custom-call | flops 1000000 | bytes 10000000 | tf_op jit(solution)/shard_map/pallas_call | solution.py:352

commit v4 on v3

--- a/solution.py
+++ b/solution.py
@@ -27,7 +27,7 @@
     n_order, n_dp, images_hbm, interp_hbm, assignment_hbm, base_hbm, counts_hbm, basis_hbm, eigen_hbm,
     cov_out, proj_out,
     assignment, counts, interp, base, images, basis, eigen, table, kept, wide, send, recv, proj, cov_own, cov_y, cov_z, cov_got,
-    image_sem, weight_sem, spec_send, spec_recv, y_send, y_recv, z_send, z_recv, proj_sem,
+    coefs, image_sem, weight_sem, spec_send, spec_recv, y_send, y_recv, z_send, z_recv, proj_sem,
 ):
     local_images, nodes, samples = images.shape
     slots = basis.shape[0]
@@ -138,7 +138,8 @@
         return wide[pl.ds(at, block), :].astype(BF16)
 
     far = len(peers) - 1
-    groups = [(0, 2), (2, per_dp)] if per_dp > 2 else [(0, per_dp)]
+    cuts = sorted({0, 1, min(3, per_dp), per_dp})
+    groups = list(zip(cuts[:-1], cuts[1:]))
     for dx in range(1, chips):
         for k0, k1 in groups:
             transform(dx, k0, k1, dx == 1 and k0 == 0)
@@ -195,32 +196,44 @@
     def proj_copy(k):
         return pltpu.make_async_copy(proj.at[k], proj_out.at[:, :, k], proj_sem.at[k])
 
-    def slot_work(k, y):
-        @pl.loop(0, half // 2)
+    side = n_order * local_images
+    batch = 4 if half % 4 == 0 else 1
+
+    def cov_work(k, y):
+        @pl.loop(0, half // batch)
         def _(h):
-            for z in (h * 2, h * 2 + 1):
-                d = z * 2 + y
-                j = d * per_dp + k
+            owners = [(h * batch + n) * 2 + y for n in range(batch)]
+            for d in owners:
                 at = pl.multiple_of(d * local_images, local_images)
                 both = jnp.concatenate(
                     [
-                        recv[k, :, p, pl.ds(at, local_images), :].reshape(
-                            n_order * local_images, nodes
-                        )
+                        recv[k, :, p, pl.ds(at, local_images), :].reshape(side, nodes)
                         for p in range(2)
                     ],
                     0,
                 )
-                coef = jnp.dot(both, kept[j], preferred_element_type=F32).astype(BF16)
-                real, imag = coef[: n_order * local_images], coef[n_order * local_images :]
+                coefs[d] = jnp.dot(
+                    both, kept[d * per_dp + k], preferred_element_type=F32
+                ).astype(BF16)
+            for n, d in enumerate(owners):
+                coef = coefs[d]
+                real, imag = coef[:side], coef[side:]
                 mixed = jnp.concatenate([real - imag, real + imag], 0)
                 cov = lax.dot_general(
                     coef, mixed, (((0,), (0,)), ((), ())), preferred_element_type=F32
                 )
-                cov_own[k, y, z] = (cov * scale).astype(BF16)
-                out = jnp.dot(coef, eigen[j], preferred_element_type=F32).astype(BF16)
-                proj[k, 0, d] = out[: n_order * local_images]
-                proj[k, 1, d] = out[n_order * local_images :]
+                cov_own[k, y, h * batch + n] = (cov * scale).astype(BF16)
+
+    def proj_work(k):
+        @pl.loop(0, n_dp // batch)
+        def _(h):
+            for n in range(batch):
+                d = h * batch + n
+                out = jnp.dot(
+                    coefs[d], eigen[d * per_dp + k], preferred_element_type=F32
+                ).astype(BF16)
+                proj[k, 0, d] = out[:side]
+                proj[k, 1, d] = out[side:]
 
     def reduce_y(k):
         y_copy(k).wait_recv()
@@ -238,12 +251,13 @@
     for k in range(per_dp):
         for t in range(len(peers)):
             spec_copy(k, t).wait_recv()
-        slot_work(k, 1 - my_y)
+        cov_work(k, 1 - my_y)
         y_copy(k).start()
-        slot_work(k, my_y)
-        proj_copy(k).start()
+        cov_work(k, my_y)
         if k >= 1:
             reduce_y(k - 1)
+        proj_work(k)
+        proj_copy(k).start()
         if k >= 2:
             reduce_z(k - 2)
     reduce_y(per_dp - 1)
@@ -323,6 +337,7 @@
             pltpu.VMEM((per_dp, half, width, width), BF16),
             pltpu.VMEM((per_dp, half, width, width), BF16),
             pltpu.VMEM((per_dp, half, width, width), BF16),
+            pltpu.VMEM((n_dp, 2 * group, width), BF16),
             dma((parts,)),
             dma((6,)),
             dma((n_peers, per_dp)),

time: 71 us -> 70.1 us (0.987)
  Pallas kernels: 70.2 us -> 69.3 us
    pallas_call x1, Pallas kernels: 67.1 us -> 66.2 us  [body(): pl.pallas_call(functools.partial(kernel, n_order, n_dp), out_shape=(jax.S...]
where the time goes in v4:
time: 70.1 us; the launch traced here: 69.9 us
  Pallas kernels  69.3 us (99%)
    pallas_call x1, Pallas kernels, body(): pl.pallas_call(functools.partial(kernel, n_order, n_dp), out_shape=(jax.S...  66.2 us
    pallas_call x1, Pallas kernels, body(): pl.pallas_call(finish, out_shape=(jax.ShapeDtypeStruct((per_dp, 2 * width...  3.05 us

profile of v4, /device:TPU:0, one launch (start us, length us, event | category | flops | bytes accessed | tf_op | source)
XLA Modules:
  0.0 69.9 jit_solution(13235970753121506665)
XLA Ops:
  0.6 66.2 %shard_map.86 = (f32[8,128,128]{2,1,0:T(8,128)S(1)}, bf16[2,8,8,128,128]{4,3,2,1,0:T(8,128)(2,1)S(1)}) custom-call(bf16[32,128,512]{2,1,0:T(8,128)(2,1)} %images_hbm.1, bf16[128,128]{1,0:T(8,128)(2,1)} %interp_hbm.1, s32[1,256]{1,0:T(1,128)} %bitcast.3, bf16[512,512]{1,0:T(8,128)(2,1)} %constant.2.clone.base_hbm, s32[64]{0:T(128)} %counts_hbm.1, ...), custom_call_target="tpu_custom_call" | custom-call | flops 5000000000 | bytes 14000000 | tf_op jit(solution)/shard_map/pallas_call | solution.py:314
  66.9 3.1 %shard_map.87 = (f32[8,32768]{1,0:T(8,128)}, bf16[2,64,128,128]{3,2,1,0:T(8,128)(2,1)}) custom-call(f32[8,128,128]{2,1,0:T(8,128)S(1)} %get-tuple-element.4.whole, bf16[2,64,128,128]{3,2,1,0:T(8,128)(2,1)S(1)} %bitcast.2), custom_call_target="tpu_custom_call" | custom-call | flops 1000000 | bytes 10000000 | tf_op jit(solution)/shard_map/pallas_call | solution.py:367

commit v5 on v4

--- a/solution.py
+++ b/solution.py
@@ -272,7 +272,7 @@
         proj_copy(k).wait()
 
 
-def finish(whole, proj, cov_out, proj_out, rows, sems):
+def finish(whole, proj, cov_out, proj_out, rows, cov, sems, cov_sems):
     parts = [(p, z) for p in range(2) for z in range(sems.shape[1])]
     size = proj.shape[1] // sems.shape[1]
     copies = [
@@ -284,13 +284,22 @@
     for copy in copies:
         copy.start()
     slots, width, _ = whole.shape
-    for k in range(slots):
-        one = whole[k]
-        flipped = one.T
-        rows[pl.ds(k, width, stride=slots), :] = (one + flipped) * 0.5
-        rows[pl.ds(width * slots + k, width, stride=slots), :] = (one - flipped) * 0.5
-    for r in range(2 * width):
-        cov_out[:, pl.ds(r * width, width)] = rows[pl.ds(r * slots, slots), :]
+    pitch = rows.shape[0] // width
+    area = width * width
+    for p in range(2):
+        for k in range(slots):
+            one = whole[k]
+            flipped = one.T
+            rows[pl.ds(k, width, stride=pitch), :] = (
+                one - flipped if p else one + flipped
+            ) * 0.5
+        for r in range(width):
+            cov[:, pl.ds(p * area + r * width, width)] = rows[pl.ds(r * pitch, slots), :]
+        copy = pltpu.make_async_copy(
+            cov.at[:, pl.ds(p * area, area)], cov_out.at[:, pl.ds(p * area, area)], cov_sems.at[p]
+        )
+        copy.start()
+        copies.append(copy)
     for copy in copies:
         copy.wait()
 
@@ -329,7 +338,7 @@
             pltpu.VMEM((slots, width, width), BF16),
             pltpu.VMEM((2, slot_total, samples), BF16),
             pltpu.VMEM((slots, nodes, width), BF16),
-            pltpu.VMEM((chip_rows * local_images, nodes), F32),
+            pltpu.VMEM(((chip_rows + 1) * local_images, nodes), F32),
             pltpu.VMEM((n_peers, per_dp, 2, block, nodes), BF16),
             pltpu.VMEM((per_dp, n_order, 2, block, nodes), BF16),
             pltpu.VMEM((per_dp, 2, n_dp, group, width), BF16),
@@ -371,8 +380,13 @@
             jax.ShapeDtypeStruct(projected.shape, BF16),
         ),
         in_specs=[vmem, any_space],
-        out_specs=(vmem, any_space),
-        scratch_shapes=[pltpu.VMEM((2 * width * per_dp, width), F32), dma((2, 4))],
+        out_specs=(any_space, any_space),
+        scratch_shapes=[
+            pltpu.VMEM((width * (per_dp + 1) + 16, width), F32),
+            pltpu.VMEM((per_dp, 2 * width * width), F32),
+            dma((2, 4)),
+            dma((2,)),
+        ],
         compiler_params=pltpu.CompilerParams(vmem_limit_bytes=16 * 2**20),
         cost_estimate=pl.CostEstimate(
             flops=1_000_000, bytes_accessed=10_000_000, transcendentals=0

time: 70.1 us -> 69.4 us (0.990)
  no operation moved by 1% of the time
where the time goes in v5:
time: 69.4 us; the launch traced here: 69.3 us
  Pallas kernels  68.6 us (99%)
    pallas_call x1, Pallas kernels, body(): pl.pallas_call(functools.partial(kernel, n_order, n_dp), out_shape=(jax.S...  66.2 us
    pallas_call x1, Pallas kernels, body(): pl.pallas_call(finish, out_shape=(jax.ShapeDtypeStruct((per_dp, 2 * width...  2.42 us

profile of v5, /device:TPU:0, one launch (start us, length us, event | category | flops | bytes accessed | tf_op | source)
XLA Modules:
  0.0 69.3 jit_solution(14699004790331103206)
XLA Ops:
  0.6 66.2 %shard_map.86 = (f32[8,128,128]{2,1,0:T(8,128)S(1)}, bf16[2,8,8,128,128]{4,3,2,1,0:T(8,128)(2,1)S(1)}) custom-call(bf16[32,128,512]{2,1,0:T(8,128)(2,1)} %images_hbm.1, bf16[128,128]{1,0:T(8,128)(2,1)} %interp_hbm.1, s32[1,256]{1,0:T(1,128)} %bitcast.3, bf16[512,512]{1,0:T(8,128)(2,1)} %constant.2.clone.base_hbm, s32[64]{0:T(128)} %counts_hbm.1, ...), custom_call_target="tpu_custom_call" | custom-call | flops 5000000000 | bytes 14000000 | tf_op jit(solution)/shard_map/pallas_call | solution.py:323
  66.9 2.4 %shard_map.87 = (f32[8,32768]{1,0:T(8,128)}, bf16[2,64,128,128]{3,2,1,0:T(8,128)(2,1)}) custom-call(f32[8,128,128]{2,1,0:T(8,128)S(1)} %get-tuple-element.4.whole, bf16[2,64,128,128]{3,2,1,0:T(8,128)(2,1)S(1)} %bitcast.2), custom_call_target="tpu_custom_call" | custom-call | flops 1000000 | bytes 10000000 | tf_op jit(solution)/shard_map/pallas_call | solution.py:376
